TPU v7x, 128 devices: a whole 4x4x4 slice. The times are simulated.
128 devices in a mesh: freq: 8 (over x, y_lo), mat: 16 (over z, y_hi, core).
Axes of the slice: x: 4, y: 4 (y_hi: 2, y_lo: 2; y = y_hi * 2 + y_lo), z: 4, core: 2. Of those that a mesh axis runs over, the one named last changes fastest.
Arguments:
- traces: bfloat16 [2048, 64, 4096], P('freq', None, 'mat'), may hold values from -6 to 6
- reflection: bfloat16 [16, 2, 4096, 4096], P('freq', None, 'mat'), may hold values from -0.0625 to 0.0625
- onset: int32 [64, 4096], P(None, 'mat'), may hold values from 512 to 2047
Outputs:
- windowed: bfloat16 [2048, 64, 4096], P('freq', None, 'mat')
Inputs may be any that keep to these rules, and one draw needn't show every extreme that they name: onset sample of the direct arrival for each focal point and receiver.
All inputs are finite; a program needn't handle non-finite values.
Results may differ from a plain program's by a relative error of at most 0.0069.
Values may be sent and summed in bfloat16 or wider, within the bound.
A program may use at most 128 MiB of HBM per device.

v0:
```python
import math
import jax
import jax.numpy as jnp
from jax import lax
from jax.sharding import PartitionSpec as P


def forward_table(base_band, first_band, band_count, sample_time_count, sampling_interval):
    angular_freq_list = base_band + first_band + jnp.arange(band_count, dtype=jnp.int32)
    sample_moments = jnp.arange(sample_time_count, dtype=jnp.int32)
    phase_angles = (
        angular_freq_list[:, None] * sample_moments[None, :] % sampling_interval
    ).astype(jnp.float32) * (2.0 * math.pi / sampling_interval)
    factor = 1.0 / math.sqrt(sampling_interval)
    table = jnp.stack([jnp.cos(phase_angles) * factor, -jnp.sin(phase_angles) * factor], axis=1)
    return table.reshape(2 * band_count, sample_time_count).astype(jnp.bfloat16)


def inverse_table(
    base_band,
    first_band,
    band_count,
    earliest_sample_time,
    sample_time_count,
    sampling_interval,
    bands_total,
):
    angular_freq_list = base_band + first_band + jnp.arange(band_count, dtype=jnp.int32)
    sample_moments = earliest_sample_time + jnp.arange(sample_time_count, dtype=jnp.int32)
    phase_angles = (
        sample_moments[:, None] * angular_freq_list[None, :] % sampling_interval
    ).astype(jnp.float32) * (2.0 * math.pi / sampling_interval)
    factor = 1.0 / math.sqrt(bands_total)
    table = jnp.stack([jnp.cos(phase_angles) * factor, -jnp.sin(phase_angles) * factor], axis=2)
    return table.reshape(sample_time_count, 2 * band_count).astype(jnp.bfloat16)


def accumulate(reflection, panels):
    return jnp.einsum("kcpw,kdrw->kcpdr", panels, reflection, preferred_element_type=jnp.float32)


def on_device(traces, reflection, onset):
    temporal_rows, focal_count, recv_rows = traces.shape
    freq_devices = lax.axis_size("freq")
    sampling_interval = temporal_rows * freq_devices
    per_device = reflection.shape[0]
    bands_total = per_device * freq_devices
    base_band = sampling_interval // 16
    earliest_sample_time = lax.axis_index("freq") * temporal_rows
    gathered = lax.all_to_all(traces, "freq", split_axis=1, concat_axis=0, tiled=True)
    forward = forward_table(base_band, 0, bands_total, sampling_interval, sampling_interval)
    local_spectra = jnp.dot(
        forward, gathered.reshape(sampling_interval, -1), preferred_element_type=jnp.float32
    )
    local_spectra = local_spectra.astype(jnp.bfloat16).reshape(
        bands_total, 2, focal_count // freq_devices, recv_rows
    )
    spectra = lax.all_to_all(local_spectra, "freq", split_axis=0, concat_axis=2, tiled=True)
    products = accumulate(reflection, lax.all_gather(spectra, "mat", axis=3, tiled=True))
    real_part = products[:, 0, :, 0] - products[:, 1, :, 1]
    imag_part = products[:, 1, :, 0] + products[:, 0, :, 1]
    response = jnp.stack([real_part, imag_part], axis=1).astype(jnp.bfloat16)
    pieces = lax.all_gather(response, "freq", axis=0, tiled=True)
    piece_bands = pieces.shape[0]
    table = inverse_table(
        base_band,
        jnp.int32(0),
        piece_bands,
        earliest_sample_time,
        temporal_rows,
        sampling_interval,
        bands_total,
    )
    wavelet_trace = jnp.dot(
        table, pieces.reshape(2 * piece_bands, -1), preferred_element_type=jnp.float32
    )
    wavelet_trace = wavelet_trace.reshape(temporal_rows, focal_count, recv_rows)
    sample_moments = earliest_sample_time + jnp.arange(temporal_rows, dtype=jnp.int32)
    return jnp.where(sample_moments[:, None, None] < onset[None], wavelet_trace, 0.0).astype(
        jnp.bfloat16
    )


def solution(mesh):
    placed = (P("freq", None, "mat"), P("freq", None, "mat", None), P(None, "mat"))
    return jax.shard_map(
        on_device, mesh=mesh, in_specs=placed, out_specs=P("freq", None, "mat"), check_vma=False
    )
```

profile of v0, /device:TPU:0, one launch (start us, length us, event | category | flops | bytes accessed | tf_op | source)
XLA Modules:
  0.0 294.2 jit_solution(8987665596310700736)
XLA Ops:
  6.5 11.5 %copy.33 = bf16[256,64,256]{2,0,1:T(8,128)(2,1)} copy(bf16[256,64,256]{2,1,0:T(8,128)(2,1)} %param.3) | data formatting | bytes 16777216 | tf_op args[0]
  18.1 5.4 %all-to-all-start = ((bf16[256,64,256]{2,0,1:T(8,128)(2,1)}), bf16[256,64,256]{2,0,1:T(8,128)(2,1)}, u32[]{:S(2)}, u32[]{:S(2)}) async-start(bf16[256,64,256]{2,0,1:T(8,128)(2,1)} %copy.33), calls=%async_computation | async-start | bytes 16777216 | tf_op jit(solution)/shard_map/all_to_all | solution.py:50
  23.5 0.2 all-gather.3.cloned.1.call-start
  23.7 0.6 multiply_convert_fusion.1
  24.3 0.1 copy.32
  24.5 0.1 convert_element_type.60
  24.5 114.7 %all-to-all-done = bf16[256,64,256]{2,0,1:T(8,128)(2,1)} async-done(((bf16[256,64,256]{2,0,1:T(8,128)(2,1)}), bf16[256,64,256]{2,0,1:T(8,128)(2,1)}, u32[]{:S(2)}, u32[]{:S(2)}) %all-to-all-start) | async-done | bytes 8388640 | tf_op jit(solution)/shard_map/all_to_all | solution.py:50
  139.3 11.9 %copy.34 = bf16[256,8,8,256]{3,2,0,1:T(8,128)(2,1)} copy(bf16[256,8,8,256]{3,0,2,1:T(8,128)(2,1)} %bitcast) | data formatting | bytes 16777216 | tf_op jit(solution)/shard_map/all_to_all | solution.py:50
  151.2 10.3 %copy.46 = bf16[256,8,8,256]{3,1,2,0:T(8,128)(2,1)} copy(bf16[256,8,8,256]{3,2,1,0:T(8,128)(2,1)} %bitcast.60) | data formatting | bytes 16777216
  161.5 4.9 %convolution_convert_fusion = bf16[32,2048]{1,0:T(8,128)(2,1)S(1)} fusion(bf16[32,2048]{1,0:T(8,128)(2,1)S(1)} %convert_element_type.60, bf16[2048,2048]{1,0:T(8,128)(2,1)} %bitcast.59), kind=kOutput, calls=%fused_computation.3 | convolution fusion | flops 268500992 | bytes 8650752 | tf_op jit(solution)/shard_map/dot_general | solution.py:52
  166.4 0.0 copy-start
  166.5 9.7 %all_to_all.33 = bf16[16,2,8,256]{3,2,1,0:T(8,128)(2,1)S(1)} all-to-all(bf16[16,2,8,256]{3,2,1,0:T(8,128)(2,1)S(1)} %bitcast.64), channel_id=1, replica_groups=mesh['freq'=8,'mat'=16] {'freq'}, dimensions={0} | all-to-all | bytes 262144 | tf_op jit(solution)/shard_map/all_to_all | solution.py:58
  176.2 0.7 copy.57
  176.8 0.0 all-gather.3.cloned.1.call-update
  176.9 0.3 all-gather.5.cloned.1.call-start
  177.1 47.8 %all-gather.3.cloned.1.call-done = bf16[2,2,64,4096]{3,2,1,0:T(8,128)(2,1)} async-done(((bf16[2,2,64,256]{3,2,1,0:T(8,128)(2,1)}), bf16[2,2,64,4096]{3,2,1,0:T(8,128)(2,1)}) %all-gather.3.cloned.1.call-update) | async-done | bytes 2097168 | tf_op jit(solution)/shard_map/all_gather | solution.py:59
  224.9 6.9 %fusion = f32[2,2,64,2,256]{4,2,3,1,0:T(8,128)S(1)} fusion(bf16[2,2,256,4096]{3,2,1,0:T(8,128)(2,1)} %param.4, bf16[2,2,64,4096]{3,2,1,0:T(8,128)(2,1)} %all-gather.3.cloned.1.call-done), kind=kOutput, calls=%fused_computation.1 | convolution fusion | flops 1073741824 | bytes 11010048 | tf_op jit(solution)/shard_map/kcpw,kdrw->kcpdr/dot_general | solution.py:39
  231.9 0.7 pad_maximum_fusion.1
  232.6 0.0 all-gather.5.cloned.1.call-update
  232.6 0.2 multiply_convert_fusion.3
  232.8 37.0 %all-gather.5.cloned.1.call-done = bf16[16,2,64,256]{3,2,0,1:T(8,128)(2,1)} async-done(((bf16[2,2,64,256]{3,2,0,1:T(8,128)(2,1)}), bf16[16,2,64,256]{3,2,0,1:T(8,128)(2,1)}) %all-gather.5.cloned.1.call-update) | async-done | bytes 1048592 | tf_op jit(solution)/shard_map/all_gather | solution.py:63
  269.8 1.3 copy.38
  271.1 0.0 copy-done
  271.1 4.7 %select_convert_fusion = bf16[256,64,256]{2,0,1:T(8,128)(2,1)} fusion(bf16[256,32,1]{0,1,2:T(8,128)(2,1)S(1)} %reshape.327, s32[64,256]{1,0:T(8,128)S(1)} %copy-done, s32[256]{0:T(256)S(1)} %iota_add_fusion, bf16[4,8,64,256]{3,2,1,0:T(8,128)(2,1)S(1)} %bitcast.61), kind=kOutput, calls=%fused_computation | convolution fusion | flops 281018368 | bytes 9520128 | tf_op jit(solution)/shard_map/dot_general | solution.py:74
  275.8 11.5 %copy.40 = bf16[256,64,256]{2,1,0:T(8,128)(2,1)} copy(bf16[256,64,256]{2,0,1:T(8,128)(2,1)} %select_convert_fusion) | data formatting | bytes 16777216 | tf_op jit(solution)/shard_map/convert_element_type | solution.py:79
  (9 shorter events, 0.1 us)
Async XLA Ops:
  18.1 121.2 %all-to-all-start = ((bf16[256,64,256]{2,0,1:T(8,128)(2,1)}), bf16[256,64,256]{2,0,1:T(8,128)(2,1)}, u32[]{:S(2)}, u32[]{:S(2)}) async-start(bf16[256,64,256]{2,0,1:T(8,128)(2,1)} %copy.33), calls=%async_computation | async-start | bytes 16777216 | tf_op jit(solution)/shard_map/all_to_all | solution.py:50
  23.5 201.4 %all-gather.3.cloned.1.call-start = ((), (), s32[]{:S(2)}) async-start(), calls=%async_computation.2 | async-start | bytes 2228224 | tf_op jit(solution)/shard_map/all_gather | solution.py:59
  166.4 104.7 %copy-start = (s32[64,256]{1,0:T(8,128)S(1)}, s32[64,256]{1,0:T(8,128)}, u32[]{:S(2)}) copy-start(s32[64,256]{1,0:T(8,128)} %param.5) | copy-start | bytes 196612
  176.9 92.9 %all-gather.5.cloned.1.call-start = ((), (), s32[]{:S(2)}) async-start(), calls=%async_computation.3 | async-start | bytes 1179648 | tf_op jit(solution)/shard_map/all_gather | solution.py:63
Sparse Core Ops, SparseCore 0:
  177.0 47.8 all-gather.2
  232.7 37.0 all-gather.4
where the time goes:
time: 295 us; the launch traced here: 294 us
  waiting for transfers between devices  200 us (68%)
  local copies, waits for them, and re-layouts  47.5 us (16%)
  matrix products  16.5 us (6%)
  between operations  13.5 us (5%)
  blocking collectives  9.71 us (3%)
  starting transfers between devices  5.88 us (2%)
    all_to_all x1, waiting for transfers between devices, on_device(): lax.all_to_all(traces, 'freq', split_axis=1, concat_axis=0, tiled=True)  115 us
    all_gather x1, waiting for transfers between devices, on_device(): lax.all_gather(spectra, 'mat', axis=3, tiled=True)  47.8 us
    all_gather x1, waiting for transfers between devices, on_device(): pieces = lax.all_gather(response, 'freq', axis=0, tiled=True)  37 us
    unnamed x5, local copies, waits for them, and re-layouts  21.9 us
    all_to_all x1, local copies, waits for them, and re-layouts, on_device(): lax.all_to_all(traces, 'freq', split_axis=1, concat_axis=0, tiled=True)  11.9 us
    convert_element_type x1, local copies, waits for them, and re-layouts, on_device(): jnp.where(sample_moments[:, None, None] < onset[None], wavelet_trace, 0.0)  11.5 us
    all_to_all x1, blocking collectives, on_device(): lax.all_to_all(local_spectra, 'freq', split_axis=0, concat_axis=2, tiled=...  9.71 us
    dot_general x1, matrix products, accumulate(): jnp.einsum('kcpw,kdrw->kcpdr', panels, reflection, preferred_element_type...  6.94 us
  transfers between devices with their start and end apart: 3, of which 3 were waited for; matrix products, arithmetic and copies ran while one was open for 0% of the time, Pallas kernels for 0%

commit v1 on v0

--- a/solution.py
+++ b/solution.py
@@ -40,6 +40,12 @@
 
 
 def on_device(traces, reflection, onset):
+
+    def _run_targets(mine, axis_id):
+        return jnp.concatenate(
+            lax.all_to_all(jnp.stack(lax.axis_size(axis_id) * [mine], 0), axis_id, 0, 0), axis=3
+        )
+
     temporal_rows, focal_count, recv_rows = traces.shape
     freq_devices = lax.axis_size("freq")
     sampling_interval = temporal_rows * freq_devices
@@ -56,7 +62,7 @@
         bands_total, 2, focal_count // freq_devices, recv_rows
     )
     spectra = lax.all_to_all(local_spectra, "freq", split_axis=0, concat_axis=2, tiled=True)
-    products = accumulate(reflection, lax.all_gather(spectra, "mat", axis=3, tiled=True))
+    products = accumulate(reflection, _run_targets(spectra, "mat"))
     real_part = products[:, 0, :, 0] - products[:, 1, :, 1]
     imag_part = products[:, 1, :, 0] + products[:, 0, :, 1]
     response = jnp.stack([real_part, imag_part], axis=1).astype(jnp.bfloat16)

time: 295 us -> 284 us (0.963)
  waiting for transfers between devices: 200 us -> 149 us
  blocking collectives: 9.71 us -> 46.7 us
  local copies, waits for them, and re-layouts: 47.5 us -> 50.7 us
    all_gather x1 -> x0, waiting for transfers between devices: 47.8 us -> none  [on_device(): lax.all_gather(spectra, 'mat', axis=3, tiled=True)]
    all_to_all x0 -> x1, blocking collectives: none -> 37 us  [_run_targets(): lax.all_to_all(jnp.stack(lax.axis_size(axis_id) * [mine], 0), axis_id, 0, 0)]
    reshape x0 -> x2, local copies, waits for them, and re-layouts: none -> 3.55 us  [_run_targets(): jnp.concatenate(lax.all_to_all(jnp.stack(lax.axis_size(axis_id) * [mine],...]
  transfers between devices with their start and end apart: 3 -> 2, of which waited for: 3 -> 2; matrix products, arithmetic and copies ran while one was open for 0% -> 0% of each run, Pallas kernels for 0% -> 0%
where the time goes in v1:
time: 284 us; the launch traced here: 283 us
  waiting for transfers between devices  149 us (52%)
  local copies, waits for them, and re-layouts  50.7 us (18%)
  blocking collectives  46.7 us (16%)
  matrix products  16.5 us (6%)
  between operations  13.5 us (5%)
  starting transfers between devices  5.61 us (2%)
    all_to_all x1, waiting for transfers between devices, on_device(): lax.all_to_all(traces, 'freq', split_axis=1, concat_axis=0, tiled=True)  115 us
    all_to_all x1, blocking collectives, _run_targets(): lax.all_to_all(jnp.stack(lax.axis_size(axis_id) * [mine], 0), axis_id, 0, 0)  37 us
    all_gather x1, waiting for transfers between devices, on_device(): pieces = lax.all_gather(response, 'freq', axis=0, tiled=True)  34 us
    unnamed x5, local copies, waits for them, and re-layouts  21.9 us
    all_to_all x1, local copies, waits for them, and re-layouts, on_device(): lax.all_to_all(traces, 'freq', split_axis=1, concat_axis=0, tiled=True)  11.9 us
    convert_element_type x1, local copies, waits for them, and re-layouts, on_device(): jnp.where(sample_moments[:, None, None] < onset[None], wavelet_trace, 0.0)  11.5 us
    all_to_all x1, blocking collectives, on_device(): lax.all_to_all(local_spectra, 'freq', split_axis=0, concat_axis=2, tiled=...  9.72 us
    dot_general x1, matrix products, accumulate(): jnp.einsum('kcpw,kdrw->kcpdr', panels, reflection, preferred_element_type...  6.94 us
  transfers between devices with their start and end apart: 2, of which 2 were waited for; matrix products, arithmetic and copies ran while one was open for 0% of the time, Pallas kernels for 0%

profile of v1, /device:TPU:0, one launch (start us, length us, event | category | flops | bytes accessed | tf_op | source)
XLA Modules:
  0.0 283.3 jit_solution(6931015237243575308)
XLA Ops:
  6.5 11.5 %copy.40 = bf16[256,64,256]{2,0,1:T(8,128)(2,1)} copy(bf16[256,64,256]{2,1,0:T(8,128)(2,1)} %param.3) | data formatting | bytes 16777216 | tf_op args[0]
  18.1 5.4 %all-to-all-start = ((bf16[256,64,256]{2,0,1:T(8,128)(2,1)}), bf16[256,64,256]{2,0,1:T(8,128)(2,1)}, u32[]{:S(2)}, u32[]{:S(2)}) async-start(bf16[256,64,256]{2,0,1:T(8,128)(2,1)} %copy.40), calls=%async_computation | async-start | bytes 16777216 | tf_op jit(solution)/shard_map/all_to_all | solution.py:56
  23.5 0.2 all-gather.2.cloned.1.call-start
  23.7 0.6 multiply_convert_fusion.1
  24.3 0.1 copy.39
  24.5 0.1 convert_element_type.60
  24.5 114.7 %all-to-all-done = bf16[256,64,256]{2,0,1:T(8,128)(2,1)} async-done(((bf16[256,64,256]{2,0,1:T(8,128)(2,1)}), bf16[256,64,256]{2,0,1:T(8,128)(2,1)}, u32[]{:S(2)}, u32[]{:S(2)}) %all-to-all-start) | async-done | bytes 8388640 | tf_op jit(solution)/shard_map/all_to_all | solution.py:56
  139.3 11.9 %copy.41 = bf16[256,8,8,256]{3,2,0,1:T(8,128)(2,1)} copy(bf16[256,8,8,256]{3,0,2,1:T(8,128)(2,1)} %bitcast) | data formatting | bytes 16777216 | tf_op jit(solution)/shard_map/all_to_all | solution.py:56
  151.2 10.3 %copy.54 = bf16[256,8,8,256]{3,1,2,0:T(8,128)(2,1)} copy(bf16[256,8,8,256]{3,2,1,0:T(8,128)(2,1)} %bitcast.61) | data formatting | bytes 16777216
  161.5 4.9 %convolution_convert_fusion = bf16[32,2048]{1,0:T(8,128)(2,1)S(1)} fusion(bf16[32,2048]{1,0:T(8,128)(2,1)S(1)} %convert_element_type.60, bf16[2048,2048]{1,0:T(8,128)(2,1)} %bitcast.60), kind=kOutput, calls=%fused_computation.3 | convolution fusion | flops 268500992 | bytes 8650752 | tf_op jit(solution)/shard_map/dot_general | solution.py:58
  166.5 9.7 %all_to_all.35 = bf16[16,2,8,256]{3,2,1,0:T(8,128)(2,1)S(1)} all-to-all(bf16[16,2,8,256]{3,2,1,0:T(8,128)(2,1)S(1)} %bitcast.66), channel_id=1, replica_groups=mesh['freq'=8,'mat'=16] {'freq'}, dimensions={0} | all-to-all | bytes 262144 | tf_op jit(solution)/shard_map/all_to_all | solution.py:64
  176.2 0.2 stack.16
  176.4 37.0 %all_to_all.36 = bf16[16,2,2,64,256]{4,3,2,1,0:T(8,128)(2,1)S(1)} all-to-all(bf16[16,2,2,64,256]{4,3,2,1,0:T(8,128)(2,1)S(1)} %stack.16), channel_id=1, replica_groups=mesh['freq'=8,'mat'=16] {'mat'}, dimensions={0} | all-to-all | bytes 4194304 | tf_op jit(solution)/shard_map/all_to_all | solution.py:46
  213.4 1.2 copy.43
  214.6 0.0 copy-start
  214.6 2.3 reshape.336
  217.0 6.9 %fusion = f32[2,2,64,2,256]{4,2,3,1,0:T(8,128)S(1)} fusion(bf16[2,2,256,4096]{3,2,1,0:T(8,128)(2,1)} %param.4, bf16[2,2,64,4096,1]{3,2,1,0,4:T(8,128)(2,1)} %reshape.336), kind=kOutput, calls=%fused_computation.1 | convolution fusion | flops 1073741824 | bytes 11010048 | tf_op jit(solution)/shard_map/kcpw,kdrw->kcpdr/dot_general | solution.py:39
  223.9 0.7 pad_maximum_fusion.1
  224.6 0.0 all-gather.2.cloned.1.call-update
  224.7 0.2 multiply_convert_fusion.3
  224.9 34.0 %all-gather.2.cloned.1.call-done = bf16[16,2,64,256]{3,2,0,1:T(8,128)(2,1)} async-done(((bf16[2,2,64,256]{3,2,0,1:T(8,128)(2,1)}), bf16[16,2,64,256]{3,2,0,1:T(8,128)(2,1)}) %all-gather.2.cloned.1.call-update) | async-done | bytes 1048592 | tf_op jit(solution)/shard_map/all_gather | solution.py:69
  258.9 1.3 copy.46
  260.2 0.0 copy-done
  260.2 4.7 %select_convert_fusion = bf16[256,64,256]{2,0,1:T(8,128)(2,1)} fusion(bf16[256,32,1]{0,1,2:T(8,128)(2,1)S(1)} %reshape.338, s32[64,256]{1,0:T(8,128)S(1)} %copy-done, s32[256]{0:T(256)S(1)} %iota_add_fusion, bf16[4,8,64,256]{3,2,1,0:T(8,128)(2,1)S(1)} %bitcast.63), kind=kOutput, calls=%fused_computation | convolution fusion | flops 281018368 | bytes 9520128 | tf_op jit(solution)/shard_map/dot_general | solution.py:80
  264.9 11.5 %copy.48 = bf16[256,64,256]{2,1,0:T(8,128)(2,1)} copy(bf16[256,64,256]{2,0,1:T(8,128)(2,1)} %select_convert_fusion) | data formatting | bytes 16777216 | tf_op jit(solution)/shard_map/convert_element_type | solution.py:85
  (10 shorter events, 0.1 us)
Async XLA Ops:
  18.1 121.2 %all-to-all-start = ((bf16[256,64,256]{2,0,1:T(8,128)(2,1)}), bf16[256,64,256]{2,0,1:T(8,128)(2,1)}, u32[]{:S(2)}, u32[]{:S(2)}) async-start(bf16[256,64,256]{2,0,1:T(8,128)(2,1)} %copy.40), calls=%async_computation | async-start | bytes 16777216 | tf_op jit(solution)/shard_map/all_to_all | solution.py:56
  23.5 235.4 %all-gather.2.cloned.1.call-start = ((), (), s32[]{:S(2)}) async-start(), calls=%async_computation.3 | async-start | bytes 1179648 | tf_op jit(solution)/shard_map/all_gather | solution.py:69
  214.6 45.6 %copy-start = (s32[64,256]{1,0:T(8,128)S(1)}, s32[64,256]{1,0:T(8,128)}, u32[]{:S(2)}) copy-start(s32[64,256]{1,0:T(8,128)} %param.5) | copy-start | bytes 196612
Sparse Core Ops, SparseCore 0:
  224.8 34.0 all-gather.1
